TPU v7x, 256 devices: a whole 4x4x8 slice. The times are simulated.
256 devices in a mesh: group: 8 (over x, core), sub: 32 (over y, z).
Axes of the slice: x: 4, y: 4, z: 8, core: 2. Of those that a mesh axis runs over, the one named last changes fastest.
Arguments:
- resid_iface: float32 [256, 16, 4352], P(('group', 'sub')), may hold values from -6 to 6
- resid_inner: float32 [256, 16, 3072], P(('group', 'sub')), may hold values from -6 to 6
- weights: float32 [256, 4352], P(('group', 'sub')), may hold values from 0.25 to 0.75
- nbr: int32 [256, 32], P(('group', 'sub')), may hold values from 0 to 1, as said below
- own2: int32 [256, 128], P(('group', 'sub')), may hold values from 0 to 2047
- cidx: int32 [256, 8], P(('group', 'sub')), may hold values from 0 to 16
- neumann: bfloat16 [256, 17, 256, 256], P(('group', 'sub'))
- dirichlet: bfloat16 [256, 8, 384, 384], P(('group', 'sub'))
- coupling: bfloat16 [256, 8, 256, 384], P(('group', 'sub')), may hold values from -0.375 to 0.375
- coarse_basis: bfloat16 [256, 4352, 128], P(('group', 'sub')), may hold values from -0.5 to 0.5
- group_basis: float32 [16384, 512], P(('group', 'sub')), may hold values from -0.25 to 0.25
- group_inverse: float32 [16384, 2048], P('group', 'sub'), as said below
- top_inverse: float32 [512, 512], replicated, as said below
Outputs:
- interface_out: float32 [256, 16, 4352], P(('group', 'sub'))
- interior_out: float32 [256, 16, 3072], P(('group', 'sub'))
Inputs may be any that keep to these rules, and one draw needn't show every extreme that they name: Symmetric within each group (nbr[(g, q), j] = nbr[(g, j), q]) with nbr[(g, q), q] = 0. `group_inverse`: each matrix of a group is symmetric. `top_inverse`: symmetric.
All inputs are finite; a program needn't handle non-finite values.
Results may differ from a plain program's by a relative error of at most 0.013.
Values may be sent and summed in bfloat16 or wider, within the bound.
A program may use at most 64 MiB of HBM per device.

v0:
```python
import jax
import jax.numpy as jnp
from jax import lax
from jax.sharding import PartitionSpec as P


def padded_2(cells, sides, width):
    for axis, dim in sides:
        count = lax.axis_size(axis)
        ends = count - 1
        head = lax.slice_in_dim(cells, 0, width, axis=dim)
        tail = lax.slice_in_dim(cells, cells.shape[dim] - width, cells.shape[dim], axis=dim)
        cells = jnp.concatenate(
            [
                lax.ppermute(tail, axis, [(i, (i + 1) % count) for i in range(ends)]),
                cells,
                lax.ppermute(head, axis, [((i + 1) % count, i) for i in range(ends)]),
            ],
            axis=dim,
        )
    return cells


def shards(
    resid_iface,
    resid_inner,
    weights,
    nbr,
    own2,
    cidx,
    neumann,
    dirichlet,
    coupling,
    coarse_basis,
    group_basis,
    group_inverse,
    top_inverse,
):
    highest = lax.Precision.HIGHEST
    nsub = lax.axis_size("sub")
    mine = lax.axis_index("sub")
    rows = resid_iface.shape[1]
    width = resid_iface.shape[2]
    slot_width = width // (nsub + 2)
    block_count = neumann.shape[1]
    block_width = neumann.shape[2]
    inner_count = dirichlet.shape[1]
    inner_width = dirichlet.shape[2]
    group_width = group_inverse.shape[0]
    share = group_inverse.shape[1]
    slot_mask = jnp.concatenate([nbr[0].astype(jnp.float32), jnp.ones((2,), jnp.float32)])
    scale = jnp.repeat(slot_mask, slot_width) * weights[0]
    weighted = (scale[None, :] * resid_iface[0]).astype(jnp.bfloat16)
    local0 = jnp.dot(weighted, coarse_basis[0], preferred_element_type=jnp.float32)
    onehot = (own2[0][:, None] == jnp.arange(group_width, dtype=jnp.int32)[None, :]).astype(
        jnp.float32
    )
    contrib = jnp.dot(local0, onehot, precision=highest)
    level2 = lax.psum(contrib.astype(jnp.bfloat16), "sub").astype(jnp.float32)
    level2_mine = lax.dynamic_slice_in_dim(level2, mine * share, share, 1)
    neumann_part = jnp.einsum(
        "rkb,kbc->rkc",
        weighted.reshape(rows, block_count, block_width),
        neumann[0],
        preferred_element_type=jnp.float32,
    ).reshape(rows, width)
    top_term = jnp.dot(level2_mine, group_basis, precision=highest)
    level3 = lax.psum(top_term, ("group", "sub"))
    coarse3 = jnp.dot(level3, top_inverse, precision=highest)
    lifted = lax.dot_general(coarse3, group_basis, (((1,), (1,)), ((), ())), precision=highest)
    coarse2_mine = jnp.dot(level2, group_inverse, precision=highest) + lifted
    coarse2 = lax.all_gather(coarse2_mine.astype(jnp.bfloat16), "sub", axis=1, tiled=True)
    values = jnp.take(coarse2, own2[0], axis=1)
    spread = lax.dot_general(
        values, coarse_basis[0], (((1,), (1,)), ((), ())), preferred_element_type=jnp.float32
    )
    scaled = scale[None, :] * (neumann_part + spread)
    slots = scaled.reshape(rows, nsub + 2, slot_width)
    received = lax.all_to_all(
        slots[:, :nsub, :].astype(jnp.bfloat16), "sub", split_axis=1, concat_axis=1, tiled=True
    ).astype(jnp.float32)
    padded = padded_2(slots[:, nsub:, :], (("group", 1),), 1)
    lower_face = slots[:, nsub, :] + padded[:, 0, :]
    upper_face = slots[:, nsub + 1, :] + padded[:, 3, :]
    total = jnp.concatenate(
        [slots[:, :nsub, :] + received, lower_face[:, None, :], upper_face[:, None, :]], axis=1
    )
    interface_out = total.reshape(rows, width)
    iface_blocks = interface_out.reshape(rows, block_count, block_width).astype(jnp.bfloat16)
    picked = jnp.take(iface_blocks, cidx[0], axis=1)
    pushed = jnp.einsum("rkb,kbc->rkc", picked, coupling[0], preferred_element_type=jnp.float32)
    inner_rhs = (resid_inner[0].reshape(rows, inner_count, inner_width) - pushed).astype(
        jnp.bfloat16
    )
    interior_out = jnp.einsum(
        "rkb,kbc->rkc", inner_rhs, dirichlet[0], preferred_element_type=jnp.float32
    ).reshape(rows, inner_count * inner_width)
    return (interface_out[None], interior_out[None])


def solution(mesh):
    placed = (
        P(("group", "sub"), None, None),
        P(("group", "sub"), None, None),
        P(("group", "sub"), None),
        P(("group", "sub"), None),
        P(("group", "sub"), None),
        P(("group", "sub"), None),
        P(("group", "sub"), None, None, None),
        P(("group", "sub"), None, None, None),
        P(("group", "sub"), None, None, None),
        P(("group", "sub"), None, None),
        P(("group", "sub"), None),
        P("group", "sub"),
        P(),
    )
    return jax.shard_map(
        shards,
        mesh=mesh,
        in_specs=placed,
        out_specs=(P(("group", "sub"), None, None), P(("group", "sub"), None, None)),
        check_vma=False,
    )
```

profile of v0, /device:TPU:1, one launch (start us, length us, event | category | flops | bytes accessed | tf_op | source)
XLA Modules:
  0.0 318.7 jit_solution(4623421728509135453)
XLA Ops:
  7.3 0.8 convert_bitcast_fusion
  8.1 0.8 fusion.45
  8.9 1.6 fusion.25
  10.5 1.8 convolution_convert_fusion
  12.6 2.0 fusion.7
  14.6 0.7 copy.43
  15.3 136.0 %all-reduce.3.cloned.1.call-done = bf16[16,2048]{1,0:T(8,128)(2,1)} async-done(((bf16[16,2048]{1,0:T(8,128)(2,1)}), bf16[16,2048]{1,0:T(8,128)(2,1)}) %all-reduce.3.cloned.1.call-update) | async-done | bytes 65552 | tf_op jit(solution)/shard_map/psum | solution.py:59
  151.3 1.7 fusion.47
  153.0 78.0 %psum.15 = f32[16,512]{1,0:T(8,128)S(1)} all-reduce(f32[16,512]{1,0:T(8,128)} %fusion.47), channel_id=1, replica_groups=mesh['group'=8,'sub'=32] {'group','sub'}, use_global_device_ids=true, to_apply=%region_1.0 | all-reduce | flops 8192 | bytes 65536 | tf_op jit(solution)/shard_map/psum | solution.py:68
  231.1 1.9 fusion.58
  233.0 1.4 fusion.57
  234.6 35.0 %all-gather = bf16[32,64,16]{1,2,0:T(8,128)(2,1)} all-gather(bf16[1,64,16]{1,2,0:T(8,128)(2,1)S(1)} %fusion.28), channel_id=1, replica_groups=mesh['group'=8,'sub'=32] {'sub'}, dimensions={0}, use_global_device_ids=true | all-gather | bytes 67584 | tf_op jit(solution)/shard_map/all_gather | solution.py:72
  269.6 1.9 copy.41
  271.5 1.8 gather_fusion
  273.3 2.2 fusion
  275.5 1.0 reshape.101
  276.5 12.7 %collective-permute-start = (f32[16,1,128]{2,1,0:T(1,128)S(1)}, f32[16,1,128]{2,1,0:T(1,128)S(1)}, u32[]{:S(2)}, u32[]{:S(2)}) collective-permute-start(f32[16,1,128]{2,1,0:T(1,128)S(1)} %get-tuple-element.4), channel_id=1, source_target_pairs={{0,32},{32,64},{64,96},{96,128},{128,160},{160,192},{192,224},{1,3... | collective-permute-start | bytes 24584 | tf_op jit(solution)/shard_map/ppermute | solution.py:15
  289.2 1.9 collective-permute-start.1
  291.9 5.6 %all-to-all-start = ((bf16[16,32,128]{2,0,1:T(8,128)(2,1)}), bf16[16,32,128]{2,0,1:T(8,128)(2,1)S(1)}, u32[]{:S(2)}, u32[]{:S(2)}) async-start(bf16[16,32,128]{2,0,1:T(8,128)(2,1)} %copy.36), calls=%async_computation | async-start | bytes 262144 | tf_op jit(solution)/shard_map/all_to_all | solution.py:79
  297.5 1.0 copy.45
  298.6 8.8 %all-to-all-done = bf16[16,32,128]{2,0,1:T(8,128)(2,1)S(1)} async-done(((bf16[16,32,128]{2,0,1:T(8,128)(2,1)}), bf16[16,32,128]{2,0,1:T(8,128)(2,1)S(1)}, u32[]{:S(2)}, u32[]{:S(2)}) %all-to-all-start) | async-done | bytes 131104 | tf_op jit(solution)/shard_map/all_to_all | solution.py:79
  308.2 2.1 fusion.10
  310.4 0.7 broadcast_in_dim_reshape.7
  311.1 0.8 broadcast_in_dim_reshape.6
  (39 shorter events, 2.1 us)
Async XLA Ops:
  7.2 301.0 %copy-start = (bf16[1,8,384,384]{3,2,1,0:T(8,128)(2,1)S(1)}, bf16[1,8,384,384]{3,2,1,0:T(8,128)(2,1)}, u32[]{:S(2)}) copy-start(bf16[1,8,384,384]{3,2,1,0:T(8,128)(2,1)} %param.20) | copy-start | bytes 7077892
  7.2 5.2 %copy-start.2 = (f32[1,16,4352]{2,1,0:T(8,128)S(1)}, f32[1,16,4352]{2,1,0:T(8,128)}, u32[]{:S(2)}) copy-start(f32[1,16,4352]{2,1,0:T(8,128)} %param.13) | copy-start | bytes 835588
  7.2 5.2 %copy-start.4 = (s32[1,128]{1,0:T(1,128)S(1)}, s32[1,128]{1,0:T(1,128)}, u32[]{:S(2)}) copy-start(s32[1,128]{1,0:T(1,128)} %param.17) | copy-start | bytes 1540
  7.2 5.3 %copy-start.5 = (s32[1,8]{1,0:T(1,128)S(1)}, s32[1,8]{1,0:T(1,128)}, u32[]{:S(2)}) copy-start(s32[1,8]{1,0:T(1,128)} %param.18) | copy-start | bytes 100
  7.2 144.1 %all-reduce.3.cloned.1.call-start = ((), (), s32[]{:S(2)}) async-start(), calls=%async_computation.1 | async-start | bytes 131072 | tf_op jit(solution)/shard_map/psum | solution.py:59
  15.3 257.9 %copy-start.1 = (bf16[1,4352,128]{2,1,0:T(8,128)(2,1)S(1)}, bf16[1,4352,128]{2,1,0:T(8,128)(2,1)}, u32[]{:S(2)}) copy-start(bf16[1,4352,128]{2,1,0:T(8,128)(2,1)} %param.22) | copy-start | bytes 3342340
  231.1 3.3 %copy-start.3 = (f32[64,512]{1,0:T(8,128)S(1)}, f32[64,512]{1,0:T(8,128)}, u32[]{:S(2)}) copy-start(f32[64,512]{1,0:T(8,128)} %param.23) | copy-start | bytes 393220
  276.5 22.0 %collective-permute-start = (f32[16,1,128]{2,1,0:T(1,128)S(1)}, f32[16,1,128]{2,1,0:T(1,128)S(1)}, u32[]{:S(2)}, u32[]{:S(2)}) collective-permute-start(f32[16,1,128]{2,1,0:T(1,128)S(1)} %get-tuple-element.4), channel_id=1, source_target_pairs={{0,32},{32,64},{64,96},{96,128},{128,160},{160,192},{192,224},{1,3... | collective-permute-start | bytes 24584 | tf_op jit(solution)/shard_map/ppermute | solution.py:15
  289.2 9.3 %collective-permute-start.1 = (f32[16,1,128]{2,1,0:T(1,128)S(1)}, f32[16,1,128]{2,1,0:T(1,128)S(1)}, u32[]{:S(2)}, u32[]{:S(2)}) collective-permute-start(f32[16,1,128]{2,1,0:T(1,128)S(1)} %get-tuple-element.5), channel_id=1, source_target_pairs={{32,0},{64,32},{96,64},{128,96},{160,128},{192,160},{224,192},{33,... | collective-permute-start | bytes 24584 | tf_op jit(solution)/shard_map/ppermute | solution.py:17
  291.9 15.5 %all-to-all-start = ((bf16[16,32,128]{2,0,1:T(8,128)(2,1)}), bf16[16,32,128]{2,0,1:T(8,128)(2,1)S(1)}, u32[]{:S(2)}, u32[]{:S(2)}) async-start(bf16[16,32,128]{2,0,1:T(8,128)(2,1)} %copy.36), calls=%async_computation | async-start | bytes 262144 | tf_op jit(solution)/shard_map/all_to_all | solution.py:79
Sparse Core Ops, SparseCore 0:
  12.5 138.7 all-reduce.2
where the time goes:
time: 319 us
  waiting for transfers between devices  145 us (45%)
  blocking collectives  113 us (35%)
  starting transfers between devices  20.3 us (6%)
  matrix products  15 us (5%)
  between operations  14.3 us (4%)
  local copies, waits for them, and re-layouts  9.48 us (3%)
    psum x1, waiting for transfers between devices, shards(): level2 = lax.psum(contrib.astype(jnp.bfloat16), 'sub').astype(jnp.float32)  136 us
    psum x1, blocking collectives, shards(): level3 = lax.psum(top_term, ('group', 'sub'))  78 us
    all_gather x1, blocking collectives, shards(): lax.all_gather(coarse2_mine.astype(jnp.bfloat16), 'sub', axis=1, tiled=True)  35 us
    ppermute x1, starting transfers between devices, padded_2(): lax.ppermute(tail, axis, [(i, (i + 1) % count) for i in range(ends)])  12.7 us
    all_to_all x1, waiting for transfers between devices, shards(): lax.all_to_all(slots[:, :nsub, :].astype(jnp.bfloat16), 'sub', split_axis...  8.85 us
  transfers between devices with their start and end apart: 4, of which 2 were waited for; matrix products, arithmetic and copies ran while one was open for 1% of the time, Pallas kernels for 0%

commit v1 on v0

--- a/solution.py
+++ b/solution.py
@@ -56,7 +56,9 @@
         jnp.float32
     )
     contrib = jnp.dot(local0, onehot, precision=highest)
-    level2 = lax.psum(contrib.astype(jnp.bfloat16), "sub").astype(jnp.float32)
+    level2 = jnp.sum(lax.all_gather(contrib.astype(jnp.bfloat16), "sub"), axis=0).astype(
+        jnp.float32
+    )
     level2_mine = lax.dynamic_slice_in_dim(level2, mine * share, share, 1)
     neumann_part = jnp.einsum(
         "rkb,kbc->rkc",

time: 319 us -> 261 us (0.82)
  waiting for transfers between devices: 145 us -> 83.9 us
    psum x1 -> x0, waiting for transfers between devices: 136 us -> none  [shards(): level2 = lax.psum(contrib.astype(jnp.bfloat16), 'sub').astype(jnp.float32)]
    all_gather x0 -> x1, waiting for transfers between devices: none -> 75 us  [shards(): lax.all_gather(contrib.astype(jnp.bfloat16), 'sub')]
  transfers between devices with their start and end apart: 4 -> 4, of which waited for: 2 -> 2; matrix products, arithmetic and copies ran while one was open for 1% -> 2% of each run, Pallas kernels for 0% -> 0%
where the time goes in v1:
time: 261 us; the launch traced here: 260 us
  blocking collectives  113 us (43%)
  waiting for transfers between devices  83.9 us (32%)
  starting transfers between devices  20.2 us (8%)
  matrix products  15.1 us (6%)
  between operations  14.3 us (5%)
  local copies, waits for them, and re-layouts  9.47 us (4%)
  other arithmetic  4.37 us (2%)
    psum x1, blocking collectives, shards(): level3 = lax.psum(top_term, ('group', 'sub'))  78.2 us
    all_gather x1, waiting for transfers between devices, shards(): lax.all_gather(contrib.astype(jnp.bfloat16), 'sub')  75 us
    all_gather x1, blocking collectives, shards(): lax.all_gather(coarse2_mine.astype(jnp.bfloat16), 'sub', axis=1, tiled=True)  34.4 us
    ppermute x1, starting transfers between devices, padded_2(): lax.ppermute(tail, axis, [(i, (i + 1) % count) for i in range(ends)])  12.5 us
    all_to_all x1, waiting for transfers between devices, shards(): lax.all_to_all(slots[:, :nsub, :].astype(jnp.bfloat16), 'sub', split_axis...  8.86 us
    all_to_all x1, starting transfers between devices, shards(): lax.all_to_all(slots[:, :nsub, :].astype(jnp.bfloat16), 'sub', split_axis...  5.8 us
  transfers between devices with their start and end apart: 4, of which 2 were waited for; matrix products, arithmetic and copies ran while one was open for 2% of the time, Pallas kernels for 0%

profile of v1, /device:TPU:1, one launch (start us, length us, event | category | flops | bytes accessed | tf_op | source)
XLA Modules:
  0.0 259.9 jit_solution(10569810040552177556)
XLA Ops:
  7.2 0.8 convert_bitcast_fusion
  8.2 0.8 fusion.45
  8.9 1.6 fusion.25
  10.5 1.8 convolution_convert_fusion
  12.5 2.0 fusion.7
  14.6 0.7 copy.43
  15.4 75.0 %all-gather.4.cloned.1.call-done = bf16[512,2048]{1,0:T(8,128)(2,1)} async-done(((bf16[16,2048]{1,0:T(8,128)(2,1)}), bf16[512,2048]{1,0:T(8,128)(2,1)}) %all-gather.4.cloned.1.call-update) | async-done | bytes 2097168 | tf_op jit(solution)/shard_map/all_gather | solution.py:59
  90.4 2.6 reduce_sum.12
  92.9 1.8 fusion.47
  94.8 78.2 %psum.7 = f32[16,512]{1,0:T(8,128)S(1)} all-reduce(f32[16,512]{1,0:T(8,128)} %fusion.47), channel_id=1, replica_groups=mesh['group'=8,'sub'=32] {'group','sub'}, use_global_device_ids=true, to_apply=%region_1.0 | all-reduce | flops 8192 | bytes 65536 | tf_op jit(solution)/shard_map/psum | solution.py:70
  172.9 1.5 fusion.57
  174.4 1.9 fusion.58
  176.5 34.4 %all-gather.1 = bf16[32,64,16]{1,2,0:T(8,128)(2,1)} all-gather(bf16[1,64,16]{1,2,0:T(8,128)(2,1)S(1)} %fusion.28), channel_id=1, replica_groups=mesh['group'=8,'sub'=32] {'sub'}, dimensions={0}, use_global_device_ids=true | all-gather | bytes 67584 | tf_op jit(solution)/shard_map/all_gather | solution.py:74
  210.9 1.9 copy.41
  212.8 1.8 gather_fusion
  214.6 2.2 fusion
  216.8 1.0 reshape.101
  217.8 12.5 %collective-permute-start = (f32[16,1,128]{2,1,0:T(1,128)S(1)}, f32[16,1,128]{2,1,0:T(1,128)S(1)}, u32[]{:S(2)}, u32[]{:S(2)}) collective-permute-start(f32[16,1,128]{2,1,0:T(1,128)S(1)} %get-tuple-element.4), channel_id=1, source_target_pairs={{0,32},{32,64},{64,96},{96,128},{128,160},{160,192},{192,224},{1,3... | collective-permute-start | bytes 24584 | tf_op jit(solution)/shard_map/ppermute | solution.py:15
  230.3 1.9 collective-permute-start.1
  232.9 5.8 %all-to-all-start = ((bf16[16,32,128]{2,0,1:T(8,128)(2,1)}), bf16[16,32,128]{2,0,1:T(8,128)(2,1)S(1)}, u32[]{:S(2)}, u32[]{:S(2)}) async-start(bf16[16,32,128]{2,0,1:T(8,128)(2,1)} %copy.36), calls=%async_computation | async-start | bytes 262144 | tf_op jit(solution)/shard_map/all_to_all | solution.py:81
  238.7 1.0 copy.45
  239.8 8.9 %all-to-all-done = bf16[16,32,128]{2,0,1:T(8,128)(2,1)S(1)} async-done(((bf16[16,32,128]{2,0,1:T(8,128)(2,1)}), bf16[16,32,128]{2,0,1:T(8,128)(2,1)S(1)}, u32[]{:S(2)}, u32[]{:S(2)}) %all-to-all-start) | async-done | bytes 131104 | tf_op jit(solution)/shard_map/all_to_all | solution.py:81
  249.4 2.1 fusion.10
  252.3 0.8 broadcast_in_dim_reshape.6
  (40 shorter events, 2.8 us)
Async XLA Ops:
  7.2 242.2 %copy-start = (bf16[1,8,384,384]{3,2,1,0:T(8,128)(2,1)S(1)}, bf16[1,8,384,384]{3,2,1,0:T(8,128)(2,1)}, u32[]{:S(2)}) copy-start(bf16[1,8,384,384]{3,2,1,0:T(8,128)(2,1)} %param.20) | copy-start | bytes 7077892
  7.2 5.2 %copy-start.2 = (f32[1,16,4352]{2,1,0:T(8,128)S(1)}, f32[1,16,4352]{2,1,0:T(8,128)}, u32[]{:S(2)}) copy-start(f32[1,16,4352]{2,1,0:T(8,128)} %param.13) | copy-start | bytes 835588
  7.2 83.2 %all-gather.4.cloned.1.call-start = ((), (), s32[]{:S(2)}) async-start(), calls=%async_computation.1 | async-start | bytes 2162688 | tf_op jit(solution)/shard_map/all_gather | solution.py:59
  12.5 2.8 %copy-start.4 = (s32[1,128]{1,0:T(1,128)S(1)}, s32[1,128]{1,0:T(1,128)}, u32[]{:S(2)}) copy-start(s32[1,128]{1,0:T(1,128)} %param.17) | copy-start | bytes 1540
  12.5 2.8 %copy-start.5 = (s32[1,8]{1,0:T(1,128)S(1)}, s32[1,8]{1,0:T(1,128)}, u32[]{:S(2)}) copy-start(s32[1,8]{1,0:T(1,128)} %param.18) | copy-start | bytes 100
  92.9 121.7 %copy-start.1 = (bf16[1,4352,128]{2,1,0:T(8,128)(2,1)S(1)}, bf16[1,4352,128]{2,1,0:T(8,128)(2,1)}, u32[]{:S(2)}) copy-start(bf16[1,4352,128]{2,1,0:T(8,128)(2,1)} %param.22) | copy-start | bytes 3342340
  172.9 3.3 %copy-start.3 = (f32[64,512]{1,0:T(8,128)S(1)}, f32[64,512]{1,0:T(8,128)}, u32[]{:S(2)}) copy-start(f32[64,512]{1,0:T(8,128)} %param.23) | copy-start | bytes 393220
  217.8 21.9 %collective-permute-start = (f32[16,1,128]{2,1,0:T(1,128)S(1)}, f32[16,1,128]{2,1,0:T(1,128)S(1)}, u32[]{:S(2)}, u32[]{:S(2)}) collective-permute-start(f32[16,1,128]{2,1,0:T(1,128)S(1)} %get-tuple-element.4), channel_id=1, source_target_pairs={{0,32},{32,64},{64,96},{96,128},{128,160},{160,192},{192,224},{1,3... | collective-permute-start | bytes 24584 | tf_op jit(solution)/shard_map/ppermute | solution.py:15
  230.3 9.4 %collective-permute-start.1 = (f32[16,1,128]{2,1,0:T(1,128)S(1)}, f32[16,1,128]{2,1,0:T(1,128)S(1)}, u32[]{:S(2)}, u32[]{:S(2)}) collective-permute-start(f32[16,1,128]{2,1,0:T(1,128)S(1)} %get-tuple-element.5), channel_id=1, source_target_pairs={{32,0},{64,32},{96,64},{128,96},{160,128},{192,160},{224,192},{33,... | collective-permute-start | bytes 24584 | tf_op jit(solution)/shard_map/ppermute | solution.py:17
  232.9 15.7 %all-to-all-start = ((bf16[16,32,128]{2,0,1:T(8,128)(2,1)}), bf16[16,32,128]{2,0,1:T(8,128)(2,1)S(1)}, u32[]{:S(2)}, u32[]{:S(2)}) async-start(bf16[16,32,128]{2,0,1:T(8,128)(2,1)} %copy.36), calls=%async_computation | async-start | bytes 262144 | tf_op jit(solution)/shard_map/all_to_all | solution.py:81
Sparse Core Ops, SparseCore 0:
  12.5 77.8 all-gather.3
